TPU v7x, 32 devices: a whole 2x2x4 slice. The times are simulated.
32 devices in a mesh: cuts: 4 (over y, core), stem: 8 (over z, x).
Axes of the slice: x: 2, y: 2, z: 4, core: 2. Of those that a mesh axis runs over, the one named last changes fastest.
Arguments:
- stem_tensor: float32 [2048, 1024], P(('cuts', 'stem')), parts along dimension 0, may hold values from -0.25 to 0.25
- stem_cotangent: float32 [2048, 1024], P(('cuts', 'stem')), parts along dimension 0, may hold values from -6 to 6
- branch_tensor: bfloat16 [1024, 1024], P('stem'), may hold values from -0.1875 to 0.1875
- bit_order: int32 [16], replicated, may hold values from 0 to 15, each once
Outputs:
- stem_grad: float32 [2048, 1024], P(('cuts', 'stem')), parts along dimension 0
- branch_grad: float32 [4096, 1024], P(('cuts', 'stem')), parts along dimension 0
There are 4 independent parts, one for each index of `cuts`. A program takes and returns all parts, laid end to end along the dimension named above; an argument that names none is the same for every part. Nothing has to cross between parts.
Inputs may be any that keep to these rules, and one draw needn't show every extreme that they name: `bit_order`: a permutation of the 16 local index bit positions.
All inputs are finite; a program needn't handle non-finite values.
Results may differ from a plain program's by a relative error of at most 0.0003.
Values may be sent and summed in bfloat16 or wider, within the bound.
A program may use at most 64 MiB of HBM per device.

v0:
```python
import jax
import jax.numpy as jnp
from jax import lax
from jax.sharding import PartitionSpec as P


def bit_tables(bit_order, local_bits, dev_bits):
    local_size = 2**local_bits
    positions = jnp.arange(local_size, dtype=jnp.int32)
    forward = jnp.zeros((local_size,), jnp.int32)
    backward = jnp.zeros((local_size,), jnp.int32)
    for order_pos in range(local_bits):
        if order_pos < dev_bits:
            target_bit = dev_bits - 1 - order_pos
        else:
            target_bit = dev_bits + local_bits - 1 - order_pos
        source = bit_order[order_pos]
        forward = forward + jnp.left_shift(jnp.right_shift(positions, source) & 1, target_bit)
        backward = backward + jnp.left_shift(jnp.right_shift(positions, target_bit) & 1, source)
    return (forward, backward)


def cross_bits(operands):
    return (lax.all_to_all(operands[0], "stem", split_axis=1, concat_axis=1, tiled=True),)


def per_device(stem_tensor, stem_cotangent, branch_tensor, bit_order):
    members = lax.axis_size("stem")
    dev_bits = members.bit_length() - 1
    row_count, width = stem_tensor.shape
    local_size = row_count * width
    local_bits = local_size.bit_length() - 1
    free_size = local_size // members
    forward, backward = bit_tables(bit_order, local_bits, dev_bits)
    arranged = jnp.take(stem_tensor.reshape(local_size), backward).reshape(free_size, members)
    gathered = lax.all_gather(branch_tensor, "stem", axis=0, tiled=True)
    adjoint = lax.dot_general(
        stem_cotangent,
        gathered.astype(jnp.float32),
        (((1,), (1,)), ((), ())),
        precision=lax.Precision.HIGHEST,
        preferred_element_type=jnp.float32,
    )
    (moved,) = cross_bits((arranged,))
    (returned,) = cross_bits((adjoint.reshape(free_size, members),))
    perm_stem = moved.reshape(row_count, width)
    branch_term = lax.dot_general(
        perm_stem,
        stem_cotangent,
        (((0,), (0,)), ((), ())),
        precision=lax.Precision.HIGHEST,
        preferred_element_type=jnp.float32,
    )
    branch_grad = lax.psum_scatter(branch_term, "stem", scatter_dimension=0, tiled=True)
    stem_grad = jnp.take(returned.reshape(local_size), forward).reshape(row_count, width)
    return (stem_grad, branch_grad)


def solution(mesh):
    placed = (P(("cuts", "stem"), None), P(("cuts", "stem"), None), P("stem", None), P())
    return jax.shard_map(
        per_device,
        mesh=mesh,
        in_specs=placed,
        out_specs=(P(("cuts", "stem"), None), P(("cuts", "stem"), None)),
        check_vma=False,
    )
```

profile of v0, /device:TPU:0, one launch (start us, length us, event | category | flops | bytes accessed | tf_op | source)
XLA Modules:
  0.0 847.5 jit_solution(13714084007219988418)
XLA Ops:
  7.2 0.0 copy-start
  7.2 0.0 all-gather.2.cloned.1.call-start
  7.2 0.7 all-gather.2.cloned.1.call-update
  7.9 0.0 reduce-scatter.2.cloned.1.call-start
  8.0 1.0 copy.10
  9.0 1.9 fusion
  10.9 10.5 %broadcast_clamp_fusion = s32[65536]{0:T(1024)S(1)} fusion(s32[]{:T(128)} %bitcast.15, s32[]{:T(128)} %bitcast.14, s32[]{:T(128)} %bitcast.13, s32[]{:T(128)} %bitcast.12, s32[]{:T(128)} %bitcast.11, s32[]{:T(128)} %bitcast.10, s32[]{:T(128)} %bitcast.9, s32[]{:T(128)} %bitcast.8, s32[]{:T(128)} %bitcast.7, s32[]{:T(128)} %bitcast.6, s32[]{:T(128)} %bitcast.5, ...), kind=kLoop, calls=%fused_computation.6 | loop fusion | flops 4390912 | bytes 262208 | tf_op gather
  21.4 362.7 %gather_fusion.1 = f32[65536]{0:T(1024)S(1)} fusion(f32[65536]{0:T(1024)S(1)} %bitcast.26, s32[65536]{0:T(1024)S(1)} %broadcast_clamp_fusion), kind=kCustom, calls=%fused_computation.1.clone | custom fusion | bytes 786432 | tf_op jit(solution)/shard_map/jit(_take)/gather | solution.py:35
  384.1 10.5 %and_select_fusion = f32[65536]{0:T(1024)S(1)} fusion(f32[65536]{0:T(1024)S(1)} %gather_fusion.1, s32[]{:T(128)} %bitcast.15, s32[]{:T(128)} %bitcast.14, s32[]{:T(128)} %bitcast.13, s32[]{:T(128)} %bitcast.12, s32[]{:T(128)} %bitcast.11, s32[]{:T(128)} %bitcast.10, s32[]{:T(128)} %bitcast.9, s32[]{:T(128)} %bitcast.8, s32[]{:T(128)} %bitcast.7, s32[]{:T(128)} %bitcast.6, ...), kind=kLoop, calls=%fused_computation.4 | loop fusion | flops 4587520 | bytes 524352 | tf_op jit(solution)/shard_map/jit(_take)/select_n | solution.py:35
  394.6 3.6 all_to_all.14
  398.2 2.8 copy.8
  401.0 16.0 %all_to_all.18 = f32[8192,8,1]{0,2,1:T(1,128)S(1)} all-to-all(f32[8192,8,1]{0,2,1:T(1,128)S(1)} %copy.8), channel_id=1, replica_groups=mesh['cuts'=4,'stem'=8] {'stem'}, dimensions={1} | all-to-all | bytes 524288 | tf_op jit(solution)/shard_map/all_to_all | solution.py:24
  417.0 2.6 copy.9
  419.5 4.0 reshape.34
  423.5 0.0 copy-done
  423.5 5.0 fusion.2
  428.6 0.0 reduce-scatter.2.cloned.1.call-update
  428.6 0.0 all-gather.2.cloned.1.call-done
  428.6 3.6 fusion.1
  432.3 3.7 all_to_all.12
  435.9 3.5 copy.6
  439.4 4.0 all-to-all-start
  443.4 10.5 %broadcast_clamp_fusion.1 = s32[65536]{0:T(1024)S(1)} fusion(s32[]{:T(128)} %bitcast.15, s32[]{:T(128)} %bitcast.14, s32[]{:T(128)} %bitcast.13, s32[]{:T(128)} %bitcast.12, s32[]{:T(128)} %bitcast.11, s32[]{:T(128)} %bitcast.10, s32[]{:T(128)} %bitcast.9, s32[]{:T(128)} %bitcast.8, s32[]{:T(128)} %bitcast.7, s32[]{:T(128)} %bitcast.6, s32[]{:T(128)} %bitcast.5, ...), kind=kLoop, calls=%fused_computation.7 | loop fusion | flops 4390912 | bytes 262208 | tf_op gather
  453.8 6.6 all-to-all-done
  460.4 2.7 copy.7
  463.1 3.7 reshape.31
  466.8 362.7 %gather_fusion = f32[65536]{0:T(1024)S(1)} fusion(f32[65536]{0:T(1024)S(1)} %reshape.31, s32[65536]{0:T(1024)S(1)} %broadcast_clamp_fusion.1), kind=kCustom, calls=%fused_computation.clone | custom fusion | bytes 786432 | tf_op jit(solution)/shard_map/jit(_take)/gather | solution.py:55
  829.5 10.5 %and_select_fusion.1 = f32[65536]{0:T(1024)S(1)} fusion(f32[65536]{0:T(1024)S(1)} %gather_fusion, s32[]{:T(128)} %bitcast.15, s32[]{:T(128)} %bitcast.14, s32[]{:T(128)} %bitcast.13, s32[]{:T(128)} %bitcast.12, s32[]{:T(128)} %bitcast.11, s32[]{:T(128)} %bitcast.10, s32[]{:T(128)} %bitcast.9, s32[]{:T(128)} %bitcast.8, s32[]{:T(128)} %bitcast.7, s32[]{:T(128)} %bitcast.6, ...), kind=kLoop, calls=%fused_computation.5 | loop fusion | flops 4587520 | bytes 524352 | tf_op jit(solution)/shard_map/jit(_take)/select_n | solution.py:55
  840.0 0.7 reshape.32
  840.7 0.0 reduce-scatter.2.cloned.1.call-done
Async XLA Ops:
  7.2 416.4 %copy-start = (f32[64,1024]{1,0:T(8,128)S(1)}, f32[64,1024]{1,0:T(8,128)}, u32[]{:S(2)}) copy-start(f32[64,1024]{1,0:T(8,128)} %param.7) | copy-start | bytes 786436
  7.2 421.5 %all-gather.2.cloned.1.call-start = ((), (), s32[]{:S(2)}) async-start(), calls=%async_computation.3 | async-start | bytes 2359296 | tf_op jit(solution)/shard_map/all_gather | solution.py:36
  7.9 832.8 %reduce-scatter.2.cloned.1.call-start = ((), (), s32[]{:S(2)}) async-start(), calls=%async_computation.4 | async-start | bytes 4718592 | tf_op jit(solution)/shard_map/reduce_scatter | solution.py:54
  439.4 21.0 %all-to-all-start = ((f32[8192,8,1]{0,2,1:T(1,128)}), f32[8192,8,1]{0,2,1:T(1,128)S(1)}, u32[]{:S(2)}, u32[]{:S(2)}) async-start(f32[8192,8,1]{0,2,1:T(1,128)} %copy.6), calls=%async_computation | async-start | bytes 524288 | tf_op jit(solution)/shard_map/all_to_all | solution.py:24
Sparse Core Ops, SparseCore 0:
  10.1 51.9 all-gather.1
  428.7 91.8 reduce-scatter.1
where the time goes:
time: 848 us
  local copies, waits for them, and re-layouts  756 us (89%)
  other arithmetic  41.9 us (5%)
  blocking collectives  16 us (2%)
  between operations  14.1 us (2%)
  matrix products  8.66 us (1%)
    gather x1, local copies, waits for them, and re-layouts, per_device(): jnp.take(stem_tensor.reshape(local_size), backward)  363 us
    gather x1, local copies, waits for them, and re-layouts, per_device(): jnp.take(returned.reshape(local_size), forward).reshape(row_count, width)  363 us
    gather x2, other arithmetic  20.9 us
    all_to_all x6, local copies, waits for them, and re-layouts, cross_bits(): lax.all_to_all(operands[0], 'stem', split_axis=1, concat_axis=1, tiled=True)  18.8 us
  transfers between devices with their start and end apart: 3, of which 1 were waited for; matrix products, arithmetic and copies ran while one was open for 94% of the time, Pallas kernels for 0%

commit v1 on v0

--- a/solution.py
+++ b/solution.py
@@ -1,7 +1,20 @@
+import functools
 import jax
 import jax.numpy as jnp
 from jax import lax
 from jax.sharding import PartitionSpec as P
+
+
+def _choose_table(x_in, axis_name, axis_no, at_axis):
+    carry_in = lax.psum(1, axis_name)
+    small = jnp.split(x_in, carry_in, axis=axis_no)
+    fresh = jnp.stack(small, axis=0)
+    block_next = lax.all_to_all(fresh, axis_name=axis_name, split_axis=0, concat_axis=0)
+    y = jnp.concatenate(block_next, axis=at_axis)
+    return y
+
+
+rest_regions = functools.partial(_choose_table, axis_name="stem", axis_no=1, at_axis=1)
 
 
 def bit_tables(bit_order, local_bits, dev_bits):
@@ -21,7 +34,7 @@
 
 
 def cross_bits(operands):
-    return (lax.all_to_all(operands[0], "stem", split_axis=1, concat_axis=1, tiled=True),)
+    return (rest_regions(operands[0]),)
 
 
 def per_device(stem_tensor, stem_cotangent, branch_tensor, bit_order):

time: 848 us -> 892 us (1.052)
  local copies, waits for them, and re-layouts: 756 us -> 806 us
  blocking collectives: 16 us -> 28.9 us
  other arithmetic: 41.9 us -> 32.3 us
    split x0 -> x2, local copies, waits for them, and re-layouts: none -> 56.8 us  [_choose_table(): small = jnp.split(x_in, carry_in, axis=axis_no)]
    all_to_all x6 -> x0, local copies, waits for them, and re-layouts: 18.8 us -> none  [cross_bits(): lax.all_to_all(operands[0], 'stem', split_axis=1, concat_axis=1, tiled=True)]
    all_to_all x1 -> x2, blocking collectives: 16 us -> 28.9 us  [_choose_table(): lax.all_to_all(fresh, axis_name=axis_name, split_axis=0, concat_axis=0)]
    gather x2 -> x1, other arithmetic: 20.9 us -> 11.2 us
  transfers between devices with their start and end apart: 3 -> 2, of which waited for: 1 -> 0; matrix products, arithmetic and copies ran while one was open for 94% -> 95% of each run, Pallas kernels for 0% -> 0%
where the time goes in v1:
time: 892 us; the launch traced here: 891 us
  local copies, waits for them, and re-layouts  806 us (90%)
  other arithmetic  32.3 us (4%)
  blocking collectives  28.9 us (3%)
  between operations  14.2 us (2%)
    gather x1, local copies, waits for them, and re-layouts, per_device(): jnp.take(stem_tensor.reshape(local_size), backward)  363 us
    gather x1, local copies, waits for them, and re-layouts, per_device(): jnp.take(returned.reshape(local_size), forward).reshape(row_count, width)  363 us
    split x2, local copies, waits for them, and re-layouts, _choose_table(): small = jnp.split(x_in, carry_in, axis=axis_no)  56.8 us
    all_to_all x2, blocking collectives, _choose_table(): lax.all_to_all(fresh, axis_name=axis_name, split_axis=0, concat_axis=0)  28.9 us
  transfers between devices with their start and end apart: 2, of which 0 were waited for; matrix products, arithmetic and copies ran while one was open for 95% of the time, Pallas kernels for 0%

profile of v1, /device:TPU:0, one launch (start us, length us, event | category | flops | bytes accessed | tf_op | source)
XLA Modules:
  0.0 891.0 jit_solution(4102315403626589164)
XLA Ops:
  7.2 0.0 copy-start
  7.2 0.0 all-gather.2.cloned.1.call-start
  7.2 0.7 all-gather.2.cloned.1.call-update
  7.9 0.0 reduce-scatter.2.cloned.1.call-start
  8.0 2.0 fusion
  9.9 1.0 copy.32
  10.9 11.2 %broadcast_clamp_fusion = (s32[65536]{0:T(1024)S(1)}, s32[65536]{0:T(1024)S(1)}) fusion(s32[]{:T(128)} %bitcast.15, s32[]{:T(128)} %bitcast.14, s32[]{:T(128)} %bitcast.13, s32[]{:T(128)} %bitcast.12, s32[]{:T(128)} %bitcast.11, s32[]{:T(128)} %bitcast.10, s32[]{:T(128)} %bitcast.9, s32[]{:T(128)} %bitcast.8, s32[]{:T(128)} %bitcast.7, s32[]{:T(128)} %bitcast.6, ...), kind=kLoop, calls=%fused_computation.22 | loop fusion | flops 8781824 | bytes 524352 | tf_op gather
  22.1 362.7 %gather_fusion.1 = f32[65536]{0:T(1024)S(1)} fusion(f32[65536]{0:T(1024)S(1)} %bitcast.44, s32[65536]{0:T(1024)S(1)} %get-tuple-element.35), kind=kCustom, calls=%fused_computation.1.clone | custom fusion | bytes 786432 | tf_op jit(solution)/shard_map/jit(_take)/gather | solution.py:48
  384.8 10.6 %and_select_fusion = f32[65536]{0:T(1024)S(1)} fusion(f32[65536]{0:T(1024)S(1)} %gather_fusion.1, s32[]{:T(128)} %bitcast.15, s32[]{:T(128)} %bitcast.14, s32[]{:T(128)} %bitcast.13, s32[]{:T(128)} %bitcast.12, s32[]{:T(128)} %bitcast.11, s32[]{:T(128)} %bitcast.10, s32[]{:T(128)} %bitcast.9, s32[]{:T(128)} %bitcast.8, s32[]{:T(128)} %bitcast.7, s32[]{:T(128)} %bitcast.6, ...), kind=kLoop, calls=%fused_computation.20 | loop fusion | flops 4587520 | bytes 524352 | tf_op jit(solution)/shard_map/jit(_take)/select_n | solution.py:48
  395.4 3.6 reshape.31
  399.0 28.3 %slice_reduce_fusion = (f32[8192]{0:T(1024)S(1)}, f32[8192]{0:T(1024)S(1)}, f32[8192]{0:T(1024)S(1)}, f32[8192]{0:T(1024)S(1)}, f32[8192]{0:T(1024)S(1)}, /*inde...) fusion(f32[8192,8]{1,0:T(8,128)} %reshape.31), kind=kLoop, calls=%fused_computation.2 | loop fusion | bytes 524288 | tf_op jit(solution)/shard_map/split | solution.py:10
  427.4 16.0 %all_to_all.10 = f32[8,8192,1]{1,2,0:T(1,128)S(1)} all-to-all(f32[8,8192,1]{1,2,0:T(1,128)S(1)} %constant_dynamic-update-slice_fusion.8), channel_id=1, replica_groups=mesh['cuts'=4,'stem'=8] {'stem'}, dimensions={0} | all-to-all | bytes 524288 | tf_op jit(solution)/shard_map/all_to_all | solution.py:12
  443.4 2.6 copy.31
  446.0 4.0 reshape_reshape.7
  450.0 0.0 copy-done
  450.0 5.1 fusion.2
  455.0 0.0 reduce-scatter.2.cloned.1.call-update
  455.1 0.0 all-gather.2.cloned.1.call-done
  455.1 3.6 fusion.1
  458.7 3.7 reshape.27
  462.4 28.4 %slice_reduce_fusion.8 = (f32[8192]{0:T(1024)S(1)}, f32[8192]{0:T(1024)S(1)}, f32[8192]{0:T(1024)S(1)}, f32[8192]{0:T(1024)S(1)}, f32[8192]{0:T(1024)S(1)}, /*in...) fusion(f32[8192,8]{1,0:T(8,128)} %reshape.27), kind=kLoop, calls=%fused_computation.10 | loop fusion | bytes 524288 | tf_op jit(solution)/shard_map/split | solution.py:10
  490.9 12.9 %all_to_all.11 = f32[8,8192,1]{1,2,0:T(1,128)S(1)} all-to-all(f32[8,8192,1]{1,2,0:T(1,128)S(1)} %constant_dynamic-update-slice_fusion), channel_id=1, replica_groups=mesh['cuts'=4,'stem'=8] {'stem'}, dimensions={0} | all-to-all | bytes 524288 | tf_op jit(solution)/shard_map/all_to_all | solution.py:12
  503.8 2.6 copy.30
  506.5 3.7 reshape_reshape.6
  510.2 362.7 %gather_fusion = f32[65536]{0:T(1024)S(1)} fusion(f32[65536]{0:T(1024)S(1)} %reshape_reshape.6, s32[65536]{0:T(1024)S(1)} %get-tuple-element.36), kind=kCustom, calls=%fused_computation.clone | custom fusion | bytes 786432 | tf_op jit(solution)/shard_map/jit(_take)/gather | solution.py:68
  872.9 10.6 %and_select_fusion.1 = f32[65536]{0:T(1024)S(1)} fusion(f32[65536]{0:T(1024)S(1)} %gather_fusion, s32[]{:T(128)} %bitcast.15, s32[]{:T(128)} %bitcast.14, s32[]{:T(128)} %bitcast.13, s32[]{:T(128)} %bitcast.12, s32[]{:T(128)} %bitcast.11, s32[]{:T(128)} %bitcast.10, s32[]{:T(128)} %bitcast.9, s32[]{:T(128)} %bitcast.8, s32[]{:T(128)} %bitcast.7, s32[]{:T(128)} %bitcast.6, ...), kind=kLoop, calls=%fused_computation.21 | loop fusion | flops 4587520 | bytes 524352 | tf_op jit(solution)/shard_map/jit(_take)/select_n | solution.py:68
  883.5 0.7 reshape.29
  884.2 0.0 reduce-scatter.2.cloned.1.call-done
  (16 shorter events, 0.2 us)
Async XLA Ops:
  7.2 442.8 %copy-start = (f32[64,1024]{1,0:T(8,128)S(1)}, f32[64,1024]{1,0:T(8,128)}, u32[]{:S(2)}) copy-start(f32[64,1024]{1,0:T(8,128)} %param.7) | copy-start | bytes 786436
  7.2 447.9 %all-gather.2.cloned.1.call-start = ((), (), s32[]{:S(2)}) async-start(), calls=%async_computation.3 | async-start | bytes 2359296 | tf_op jit(solution)/shard_map/all_gather | solution.py:49
  7.9 876.3 %reduce-scatter.2.cloned.1.call-start = ((), (), s32[]{:S(2)}) async-start(), calls=%async_computation.4 | async-start | bytes 4718592 | tf_op jit(solution)/shard_map/reduce_scatter | solution.py:67
Sparse Core Ops, SparseCore 0:
  10.1 52.1 all-gather.1
  455.2 89.7 reduce-scatter.1
